TPU v7x, 512 devices: a whole 4x4x16 slice. The times are simulated.
512 devices in a mesh: dp: 2 (over core), fsdp: 32 (over y, z_lo), tensor: 8 (over z_hi, x).
Axes of the slice: x: 4, y: 4, z: 16 (z_hi: 2, z_lo: 8; z = z_hi * 8 + z_lo), core: 2. Of those that a mesh axis runs over, the one named last changes fastest.
Arguments:
- tokens: bfloat16 [16384, 4096], P(('dp', 'fsdp', 'tensor')), may hold values from -40 to 40
- norm_gain: float32 [4096], replicated, may hold values from 0.5 to 1.5
- tile_values: bfloat16 [512, 128, 128], P(('fsdp', 'tensor')), may hold values from -0.25 to 0.25
- tile_rows: int32 [8, 64], P('tensor'), may hold values from 0 to 31, as said below
- tile_cols: int32 [8, 64], P('tensor'), may hold values from 0 to 13
- tile_counts: int32 [8, 32], P('tensor'), may hold values from 0 to 2, as said below
- grad_out: bfloat16 [16384, 14336], P(('dp', 'fsdp'), 'tensor'), may hold values from -3 to 3
Outputs:
- mixed: bfloat16 [16384, 14336], P(('dp', 'fsdp'), 'tensor')
- grad_x: bfloat16 [16384, 4096], P(('dp', 'fsdp', 'tensor'))
- grad_gain: float32 [4096], replicated
- grad_tiles: float32 [512, 128, 128], P(('fsdp', 'tensor'))
Inputs may be any that keep to these rules, and one draw needn't show every extreme that they name: `tile_counts`: for each tensor index the counts over the 32 fsdp shards sum to 56, and some shard holds exactly 2. `tile_rows`: within one tensor index the (row, column) pairs of held slots are all different.
All inputs are finite; a program needn't handle non-finite values.
Results may differ from a plain program's by a relative error of at most 0.013.
Values may be sent and summed in bfloat16 or wider, within the bound.
A program may use at most 128 MiB of HBM per device.

v0:
```python
import jax
import jax.numpy as jnp
from jax import lax
from jax.sharding import PartitionSpec as P


def tile_forward(group_rows, values, rows_list, cols_list, col_tiles):
    tile_size = values.shape[1]
    blocks = group_rows.reshape(group_rows.shape[0], -1, tile_size)
    picked = jnp.take(blocks, rows_list, axis=1)
    product = jnp.einsum("tsk,skn->tsn", picked, values, preferred_element_type=jnp.float32)
    placed = (
        jnp.zeros((group_rows.shape[0], col_tiles, tile_size), jnp.float32)
        .at[:, cols_list]
        .add(product)
    )
    return placed.reshape(group_rows.shape[0], col_tiles * tile_size)


def tile_backward(grad_rows, values, rows_list, cols_list, row_tiles):
    tile_size = values.shape[1]
    blocks = grad_rows.reshape(grad_rows.shape[0], -1, tile_size)
    picked = jnp.take(blocks, cols_list, axis=1)
    product = jnp.einsum("tsn,skn->tsk", picked, values, preferred_element_type=jnp.float32)
    placed = (
        jnp.zeros((grad_rows.shape[0], row_tiles, tile_size), jnp.float32)
        .at[:, rows_list]
        .add(product)
    )
    return placed.reshape(grad_rows.shape[0], row_tiles * tile_size)


def per_device(tokens, norm_gain, tile_values, tile_rows, tile_cols, tile_counts, grad_out):
    tile_size = tile_values.shape[1]
    slot_cap = tile_values.shape[0]
    row_tiles = tokens.shape[1] // tile_size
    col_tiles = grad_out.shape[1] // tile_size
    rows_list = tile_rows[0]
    cols_list = tile_cols[0]
    shard_counts = tile_counts[0]
    held_all = (jnp.arange(slot_cap)[None, :] < shard_counts[:, None]).reshape(-1)
    own_held = jnp.arange(slot_cap) < shard_counts[lax.axis_index("fsdp")]
    local_float = tokens.astype(jnp.float32)
    inv_rms = lax.rsqrt(jnp.mean(local_float * local_float, axis=1, keepdims=True) + 1e-05)
    scaled = local_float * inv_rms
    normed = (scaled * norm_gain).astype(jnp.bfloat16)
    group_rows = lax.all_gather(normed, "tensor", axis=0, tiled=True)
    gathered = lax.all_gather(tile_values, "fsdp", axis=0, tiled=True)
    kept_values = jnp.where(held_all[:, None, None], gathered, jnp.zeros_like(gathered))
    outputs = tile_forward(group_rows, kept_values, rows_list, cols_list, col_tiles)
    mixed = outputs.astype(jnp.bfloat16)
    input_grad = lax.psum_scatter(
        tile_backward(grad_out, kept_values, rows_list, cols_list, row_tiles).astype(jnp.bfloat16),
        "tensor",
        scatter_dimension=0,
        tiled=True,
    ).astype(jnp.float32)
    x_blocks = group_rows.reshape(group_rows.shape[0], row_tiles, tile_size)
    g_blocks = grad_out.reshape(grad_out.shape[0], col_tiles, tile_size)
    picked_x = jnp.take(x_blocks, rows_list, axis=1)
    picked_g = jnp.take(g_blocks, cols_list, axis=1)
    grad_shard = lax.psum_scatter(
        jnp.einsum("tsk,tsn->skn", picked_x, picked_g, preferred_element_type=jnp.float32),
        "fsdp",
        scatter_dimension=0,
        tiled=True,
    )
    grad_shard = jnp.where(own_held[:, None, None], grad_shard, jnp.zeros_like(grad_shard))
    grad_tiles = lax.psum(grad_shard, "dp")
    gain_part = jnp.sum(input_grad * scaled, axis=0)
    grad_gain = lax.psum(gain_part, ("dp", "fsdp", "tensor"))
    hidden_grad = input_grad * norm_gain
    grad_x = (
        inv_rms * (hidden_grad - scaled * jnp.mean(hidden_grad * scaled, axis=1, keepdims=True))
    ).astype(jnp.bfloat16)
    return (mixed, grad_x, grad_gain, grad_tiles)


def solution(mesh):
    placed = (
        P(("dp", "fsdp", "tensor"), None),
        P(),
        P(("fsdp", "tensor"), None, None),
        P("tensor", None),
        P("tensor", None),
        P("tensor", None),
        P(("dp", "fsdp"), "tensor"),
    )
    return jax.shard_map(
        per_device,
        mesh=mesh,
        in_specs=placed,
        out_specs=(
            P(("dp", "fsdp"), "tensor"),
            P(("dp", "fsdp", "tensor"), None),
            P(),
            P(("fsdp", "tensor"), None, None),
        ),
        check_vma=False,
    )
```

profile of v0, /device:TPU:1, one launch (start us, length us, event | category | flops | bytes accessed | tf_op | source)
XLA Modules:
  0.0 848.5 jit_solution(9026113694259479338)
XLA Ops:
  7.2 0.0 all-gather.3.cloned.1.call-start
  7.2 0.7 all-gather.3.cloned.1.call-update
  7.9 0.0 reduce-scatter.7.cloned.1.call-start
  7.9 1.5 copy.32
  9.4 0.6 copy.33
  10.0 0.7 iota_compare_fusion
  10.8 0.1 lt.72
  10.9 0.7 compare_select_fusion
  11.6 0.0 copy-start.5
  11.6 3.1 gather_fusion.1
  14.6 0.0 copy-done.4
  14.7 207.7 %all-gather.3.cloned.1.call-done = bf16[64,128,128]{2,1,0:T(8,128)(2,1)} async-done(((bf16[2,128,128]{2,1,0:T(8,128)(2,1)}), bf16[64,128,128]{2,1,0:T(8,128)(2,1)}) %all-gather.3.cloned.1.call-update) | async-done | bytes 2097168 | tf_op jit(solution)/shard_map/all_gather | solution.py:48
  222.3 7.4 fusion.2
  229.8 2.4 broadcast_in_dim.57
  232.2 19.4 %scatter_fusion.1 = f32[256,32,128]{2,0,1:T(8,128)} fusion(f32[256,32,128]{2,0,1:T(8,128)} %broadcast_in_dim.57, s32[64]{0:T(128)S(1)} %fusion.18, f32[64,256,128]{2,1,0:T(8,128)} %fusion.2), kind=kCustom, calls=%fused_computation.3 | custom fusion | flops 2097152 | bytes 25166080 | tf_op jit(solution)/shard_map/scatter-add | solution.py:28
  251.6 2.5 convert_element_type.28
  254.1 2.9 copy.34
  257.0 4.1 copy.39
  261.2 0.0 reduce-scatter.7.cloned.1.call-update
  261.2 0.0 all-gather.5.cloned.1.call-start
  261.2 0.2 fusion.15
  261.4 162.8 %reduce-scatter.7.cloned.1.call-done = bf16[32,4096]{1,0:T(8,128)(2,1)} async-done(((bf16[256,4096]{1,0:T(8,128)(2,1)}), bf16[32,4096]{1,0:T(8,128)(2,1)}) %reduce-scatter.7.cloned.1.call-update) | async-done | bytes 262160 | tf_op jit(solution)/shard_map/reduce_scatter | solution.py:52
  424.3 1.3 fusion.16
  425.5 1.9 fusion.12
  427.5 0.0 all-gather.5.cloned.1.call-update
  427.5 0.0 reduce-scatter.5.cloned.1.call-start
  427.6 109.9 %all-gather.5.cloned.1.call-done = bf16[256,4096]{1,0:T(8,128)(2,1)} async-done(((bf16[32,4096]{1,0:T(8,128)(2,1)}), bf16[256,4096]{1,0:T(8,128)(2,1)}) %all-gather.5.cloned.1.call-update) | async-done | bytes 2097168 | tf_op jit(solution)/shard_map/all_gather | solution.py:47
  537.5 4.1 copy.29
  541.6 3.2 copy.30
  544.8 3.0 gather_fusion
  547.8 7.0 fusion
  554.8 0.0 reduce-scatter.5.cloned.1.call-update
  554.9 0.0 all-reduce.2.cloned.1.call-start
  554.9 0.6 copy-done.3
  555.5 0.6 constant_dynamic-slice_fusion
  556.1 0.6 iota_compare_fusion.1
  556.7 103.2 %psum.14 = f32[4096]{0:T(1024)} all-reduce(f32[4096]{0:T(1024)S(1)} %get-tuple-element.18), channel_id=1, replica_groups=mesh['dp'=2,'fsdp'=32,'tensor'=8] {'dp','fsdp','tensor'}, use_global_device_ids=true, to_apply=%region_6.9 | all-reduce | flops 4096 | bytes 32768 | tf_op jit(solution)/shard_map/psum | solution.py:71
  659.9 119.5 %reduce-scatter.5.cloned.1.call-done = f32[2,128,128]{2,1,0:T(8,128)} async-done(((f32[64,128,128]{2,1,0:T(8,128)}), f32[2,128,128]{2,1,0:T(8,128)}) %reduce-scatter.5.cloned.1.call-update) | async-done | bytes 131088 | tf_op jit(solution)/shard_map/reduce_scatter | solution.py:62
  779.5 1.6 broadcast_select_fusion.9
  781.1 0.0 all-reduce.2.cloned.1.call-update
  781.1 6.7 fusion.5
  787.9 0.2 broadcast_in_dim.54
  788.0 12.4 %scatter_fusion = f32[256,14,128]{2,0,1:T(8,128)S(1)} fusion(f32[256,14,128]{2,0,1:T(8,128)S(1)} %broadcast_in_dim.54, s32[64]{0:T(128)S(1)} %fusion.17, f32[64,256,128]{2,1,0:T(8,128)} %fusion.5), kind=kCustom, calls=%fused_computation.2 | custom fusion | flops 2097152 | bytes 25166080 | tf_op jit(solution)/shard_map/scatter-add | solution.py:15
  800.5 0.2 convert_element_type.26
  800.6 0.5 copy.31
  801.2 1.4 copy.37
  802.5 37.8 %all-reduce.2.cloned.1.call-done = f32[2,128,128]{2,1,0:T(8,128)} async-done(((f32[2,128,128]{2,1,0:T(8,128)}), f32[2,128,128]{2,1,0:T(8,128)}) %all-reduce.2.cloned.1.call-update) | async-done | bytes 131088 | tf_op jit(solution)/shard_map/psum | solution.py:69
  840.4 1.6 copy.44
  (17 shorter events, 0.1 us)
Async XLA Ops:
  7.2 215.2 %all-gather.3.cloned.1.call-start = ((), (), s32[]{:S(2)}) async-start(), calls=%async_computation.2 | async-start | bytes 2162688 | tf_op jit(solution)/shard_map/all_gather | solution.py:48
  7.9 416.4 %reduce-scatter.7.cloned.1.call-start = ((), (), s32[]{:S(2)}) async-start(), calls=%async_computation.6 | async-start | bytes 2359296 | tf_op jit(solution)/shard_map/reduce_scatter | solution.py:52
  11.6 3.1 copy-start.4
  11.6 3.1 copy-start.5
  257.0 4.2 copy-start.1
  257.0 167.2 %copy-start.2 = (f32[4096]{0:T(1024)S(1)}, f32[4096]{0:T(1024)}, u32[]{:S(2)}) copy-start(f32[4096]{0:T(1024)} %param.12) | copy-start | bytes 49156
  261.2 276.3 %all-gather.5.cloned.1.call-start = ((), (), s32[]{:S(2)}) async-start(), calls=%async_computation.3 | async-start | bytes 2359296 | tf_op jit(solution)/shard_map/all_gather | solution.py:47
  427.5 352.0 %reduce-scatter.5.cloned.1.call-start = ((), (), s32[]{:S(2)}) async-start(), calls=%async_computation.4 | async-start | bytes 4325376 | tf_op jit(solution)/shard_map/reduce_scatter | solution.py:62
  554.8 0.7 copy-start.3
  554.8 226.3 %copy-start = (bf16[64,128,128]{2,1,0:T(8,128)(2,1)S(1)}, bf16[64,128,128]{2,1,0:T(8,128)(2,1)}, u32[]{:S(2)}) copy-start(bf16[64,128,128]{2,1,0:T(8,128)(2,1)} %all-gather.3.cloned.1.call-done) | copy-start | bytes 6291460
  554.9 285.5 %all-reduce.2.cloned.1.call-start = ((), (), s32[]{:S(2)}) async-start(), calls=%async_computation.5 | async-start | bytes 262144 | tf_op jit(solution)/shard_map/psum | solution.py:69
Sparse Core Ops, SparseCore 0:
  10.1 212.2 all-gather.2
  261.3 162.8 reduce-scatter.6
  428.5 108.9 all-gather.4
  555.0 224.4 reduce-scatter.4
  783.0 57.3 all-reduce.1
where the time goes:
time: 849 us; the launch traced here: 848 us
  waiting for transfers between devices  639 us (75%)
  blocking collectives  103 us (12%)
  other arithmetic  41.6 us (5%)
  local copies, waits for them, and re-layouts  29.9 us (4%)
  matrix products  21.2 us (2%)
  between operations  13.9 us (2%)
    all_gather x1, waiting for transfers between devices, per_device(): gathered = lax.all_gather(tile_values, 'fsdp', axis=0, tiled=True)  208 us
    reduce_scatter x1, waiting for transfers between devices, per_device(): lax.psum_scatter(tile_backward(grad_out, kept_values, rows_list, cols_lis...  163 us
    reduce_scatter x1, waiting for transfers between devices, per_device(): lax.psum_scatter(jnp.einsum('tsk,tsn->skn', picked_x, picked_g, preferred...  120 us
    all_gather x1, waiting for transfers between devices, per_device(): group_rows = lax.all_gather(normed, 'tensor', axis=0, tiled=True)  110 us
    psum x1, blocking collectives, per_device(): grad_gain = lax.psum(gain_part, ('dp', 'fsdp', 'tensor'))  103 us
    psum x1, waiting for transfers between devices, per_device(): grad_tiles = lax.psum(grad_shard, 'dp')  37.8 us
    scatter-add x1, other arithmetic, tile_backward(): placed = jnp.zeros((grad_rows.shape[0], row_tiles, tile_size), jnp.float3...  19.4 us
  transfers between devices with their start and end apart: 5, of which 5 were waited for; matrix products, arithmetic and copies ran while one was open for 3% of the time, Pallas kernels for 0%

commit v1 on v0

--- a/solution.py
+++ b/solution.py
@@ -68,7 +68,7 @@
     grad_shard = jnp.where(own_held[:, None, None], grad_shard, jnp.zeros_like(grad_shard))
     grad_tiles = lax.psum(grad_shard, "dp")
     gain_part = jnp.sum(input_grad * scaled, axis=0)
-    grad_gain = lax.psum(gain_part, ("dp", "fsdp", "tensor"))
+    grad_gain = lax.psum(lax.psum(gain_part, "dp"), ("fsdp", "tensor"))
     hidden_grad = input_grad * norm_gain
     grad_x = (
         inv_rms * (hidden_grad - scaled * jnp.mean(hidden_grad * scaled, axis=1, keepdims=True))

time: 849 us -> 2670 us (3.14)
  blocking collectives: 103 us -> 1830 us
  waiting for transfers between devices: 639 us -> 736 us
    psum x1 -> x2, blocking collectives: 103 us -> 1830 us  [per_device(): grad_gain = lax.psum(lax.psum(gain_part, 'dp'), ('fsdp', 'tensor'))]
    psum x1, waiting for transfers between devices: 37.8 us -> 255 us  [per_device(): grad_tiles = lax.psum(grad_shard, 'dp')]
    reduce_scatter x1, waiting for transfers between devices: 120 us -> 0.01 us  [per_device(): lax.psum_scatter(jnp.einsum('tsk,tsn->skn', picked_x, picked_g, preferred...]
  transfers between devices with their start and end apart: 5 -> 5, of which waited for: 5 -> 4; matrix products, arithmetic and copies ran while one was open for 3% -> 1% of each run, Pallas kernels for 0% -> 0%
where the time goes in v1:
time: 2670 us
  blocking collectives  1830 us (69%)
  waiting for transfers between devices  736 us (28%)
  other arithmetic  41.6 us (2%)
  local copies, waits for them, and re-layouts  29.9 us (1%)
    psum x2, blocking collectives, per_device(): grad_gain = lax.psum(lax.psum(gain_part, 'dp'), ('fsdp', 'tensor'))  1830 us
    psum x1, waiting for transfers between devices, per_device(): grad_tiles = lax.psum(grad_shard, 'dp')  255 us
    all_gather x1, waiting for transfers between devices, per_device(): gathered = lax.all_gather(tile_values, 'fsdp', axis=0, tiled=True)  208 us
    reduce_scatter x1, waiting for transfers between devices, per_device(): lax.psum_scatter(tile_backward(grad_out, kept_values, rows_list, cols_lis...  163 us
    all_gather x1, waiting for transfers between devices, per_device(): group_rows = lax.all_gather(normed, 'tensor', axis=0, tiled=True)  110 us
  transfers between devices with their start and end apart: 5, of which 4 were waited for; matrix products, arithmetic and copies ran while one was open for 1% of the time, Pallas kernels for 0%

profile of v1, /device:TPU:1, one launch (start us, length us, event | category | flops | bytes accessed | tf_op | source)
XLA Modules:
  0.0 2668.8 jit_solution(11433064209790548050)
XLA Ops:
  7.2 0.0 all-gather.3.cloned.1.call-start
  7.2 0.7 all-gather.3.cloned.1.call-update
  7.9 0.0 reduce-scatter.7.cloned.1.call-start
  7.9 1.5 copy.32
  9.4 0.6 copy.33
  10.0 0.7 iota_compare_fusion
  10.8 0.1 lt.72
  10.9 0.7 compare_select_fusion
  11.6 0.0 copy-start.5
  11.6 3.1 gather_fusion.1
  14.6 0.0 copy-done.4
  14.7 207.7 %all-gather.3.cloned.1.call-done = bf16[64,128,128]{2,1,0:T(8,128)(2,1)} async-done(((bf16[2,128,128]{2,1,0:T(8,128)(2,1)}), bf16[64,128,128]{2,1,0:T(8,128)(2,1)}) %all-gather.3.cloned.1.call-update) | async-done | bytes 2097168 | tf_op jit(solution)/shard_map/all_gather | solution.py:48
  222.3 7.4 fusion.2
  229.8 2.4 broadcast_in_dim.57
  232.2 19.4 scatter_fusion.1
  251.6 2.5 convert_element_type.28
  254.1 2.9 copy.34
  257.0 4.1 copy.39
  261.2 0.0 reduce-scatter.7.cloned.1.call-update
  261.2 0.0 all-gather.5.cloned.1.call-start
  261.3 0.2 fusion.15
  261.4 163.2 %reduce-scatter.7.cloned.1.call-done = bf16[32,4096]{1,0:T(8,128)(2,1)} async-done(((bf16[256,4096]{1,0:T(8,128)(2,1)}), bf16[32,4096]{1,0:T(8,128)(2,1)}) %reduce-scatter.7.cloned.1.call-update) | async-done | bytes 262160 | tf_op jit(solution)/shard_map/reduce_scatter | solution.py:52
  424.6 1.3 fusion.16
  425.9 1.9 fusion.12
  427.9 0.0 all-gather.5.cloned.1.call-update
  427.9 0.0 reduce-scatter.5.cloned.1.call-start
  428.0 109.9 %all-gather.5.cloned.1.call-done = bf16[256,4096]{1,0:T(8,128)(2,1)} async-done(((bf16[32,4096]{1,0:T(8,128)(2,1)}), bf16[256,4096]{1,0:T(8,128)(2,1)}) %all-gather.5.cloned.1.call-update) | async-done | bytes 2097168 | tf_op jit(solution)/shard_map/all_gather | solution.py:47
  537.8 4.1 copy.29
  541.9 3.2 copy.30
  545.1 3.0 gather_fusion
  548.2 7.0 fusion
  555.2 0.0 reduce-scatter.5.cloned.1.call-update
  555.2 0.0 all-reduce.2.cloned.1.call-start
  555.3 0.6 copy-done.3
  555.8 0.6 constant_dynamic-slice_fusion
  556.4 0.6 iota_compare_fusion.1
  557.1 5.4 psum.21
  562.5 1820.2 %psum.22 = f32[4096]{0:T(1024)} all-reduce(f32[4096]{0:T(1024)S(1)} %psum.21), channel_id=1, replica_groups=mesh['dp'=2,'fsdp'=32,'tensor'=8] {'fsdp','tensor'}, use_global_device_ids=true, to_apply=%region_7.10 | all-reduce | flops 4096 | bytes 32768 | tf_op jit(solution)/shard_map/psum | solution.py:71
  2382.7 1.6 broadcast_select_fusion.9
  2384.3 0.0 all-reduce.2.cloned.1.call-update
  2384.4 6.7 fusion.5
  2391.1 0.2 broadcast_in_dim.54
  2391.3 12.4 scatter_fusion
  2403.7 0.2 convert_element_type.26
  2403.9 0.5 copy.31
  2404.4 1.4 copy.37
  2405.8 254.9 %all-reduce.2.cloned.1.call-done = f32[2,128,128]{2,1,0:T(8,128)} async-done(((f32[2,128,128]{2,1,0:T(8,128)}), f32[2,128,128]{2,1,0:T(8,128)}) %all-reduce.2.cloned.1.call-update) | async-done | bytes 131088 | tf_op jit(solution)/shard_map/psum | solution.py:69
  2660.7 1.6 copy.44
  (18 shorter events, 0.1 us)
Async XLA Ops:
  7.2 215.2 %all-gather.3.cloned.1.call-start = ((), (), s32[]{:S(2)}) async-start(), calls=%async_computation.2 | async-start | bytes 2162688 | tf_op jit(solution)/shard_map/all_gather | solution.py:48
  7.9 416.7 %reduce-scatter.7.cloned.1.call-start = ((), (), s32[]{:S(2)}) async-start(), calls=%async_computation.6 | async-start | bytes 2359296 | tf_op jit(solution)/shard_map/reduce_scatter | solution.py:52
  11.6 3.1 copy-start.4
  11.6 3.1 copy-start.5
  257.0 4.2 copy-start.1
  257.0 167.6 %copy-start.2 = (f32[4096]{0:T(1024)S(1)}, f32[4096]{0:T(1024)}, u32[]{:S(2)}) copy-start(f32[4096]{0:T(1024)} %param.12) | copy-start | bytes 49156
  261.2 276.6 %all-gather.5.cloned.1.call-start = ((), (), s32[]{:S(2)}) async-start(), calls=%async_computation.3 | async-start | bytes 2359296 | tf_op jit(solution)/shard_map/all_gather | solution.py:47
  427.9 1954.8 %reduce-scatter.5.cloned.1.call-start = ((), (), s32[]{:S(2)}) async-start(), calls=%async_computation.4 | async-start | bytes 4325376 | tf_op jit(solution)/shard_map/reduce_scatter | solution.py:62
  555.2 0.7 copy-start.3
  555.2 1829.2 %copy-start = (bf16[64,128,128]{2,1,0:T(8,128)(2,1)S(1)}, bf16[64,128,128]{2,1,0:T(8,128)(2,1)}, u32[]{:S(2)}) copy-start(bf16[64,128,128]{2,1,0:T(8,128)(2,1)} %all-gather.3.cloned.1.call-done) | copy-start | bytes 6291460
  555.2 2105.5 %all-reduce.2.cloned.1.call-start = ((), (), s32[]{:S(2)}) async-start(), calls=%async_computation.5 | async-start | bytes 262144 | tf_op jit(solution)/shard_map/psum | solution.py:69
Sparse Core Ops, SparseCore 0:
  10.1 212.2 all-gather.2
  261.3 163.2 reduce-scatter.6
  428.9 108.8 all-gather.4
  555.3 224.8 reduce-scatter.4
  2384.5 276.1 all-reduce.1
